TPU v7x, 32 devices: a whole 2x2x4 slice. The times are simulated.
32 devices in a mesh: comp: 2 (over x), row: 4 (over z), col: 4 (over y, core).
Axes of the slice: x: 2, y: 2, z: 4, core: 2. Of those that a mesh axis runs over, the one named last changes fastest.
Arguments:
- column: float32 [2, 8, 128, 512], P('comp', None, 'row', 'col'), may hold values from -6 to 6
- fast_state: float32 [2, 3, 128, 512], P('comp', None, 'row', 'col'), may hold values from -6 to 6
- wave_depth: float32 [2, 128, 512], P('comp', 'row', 'col'), may hold values from 0.5 to 2
- wet_mask: int32 [2, 128, 512], P('comp', 'row', 'col'), may hold values 0 or 1
- surface: float32 [2, 8, 128, 512], P('comp', None, 'row', 'col'), may hold values from -6 to 6
- coupling: float32 [2, 11, 8], P('comp'), may hold values from -2 to 2
- emission: float32 [2, 8, 11], P('comp'), may hold values from -1.75 to 1.75
- remap_weight: bfloat16 [2, 128, 16, 4, 128], P('comp', 'row', 'col'), may hold values from -1.5 to 1.5
- send_block: int32 [2, 4, 16, 32], P('comp', 'row', 'col'), may hold values from 0 to 31
- link_slot: int32 [2, 4, 512], P('comp', 'row', 'col'), may hold values from 0 to 127, as said below
Outputs:
- new_column: float32 [2, 8, 128, 512], P('comp', None, 'row', 'col')
- fast_final: float32 [2, 3, 128, 512], P('comp', None, 'row', 'col')
- next_surface: float32 [2, 8, 128, 512], P('comp', None, 'row', 'col')
Inputs may be any that keep to these rules, and one draw needn't show every extreme that they name: `send_block`: each entry names a latitude row of the sending device's tile. `link_slot`: on each device the 128 links read every received slot exactly once.
All inputs are finite; a program needn't handle non-finite values. No bound on the sum of `wet_mask` on one device may be relied on, other than what follows from the above.
Results may differ from a plain program's by a relative error of at most 0.0023.
Values may be sent and summed in bfloat16 or wider, within the bound.
A program may use at most 64 MiB of HBM per device.

v0:
```python
import jax
import jax.numpy as jnp
from jax import lax
from jax.sharding import PartitionSpec as P

H = 32
W = 128
K = 4
Q = 8
SUBSTEPS = 32


STEP_SIZE = 0.35
DAMPING = 0.97


def swapped(block, axis, bit):
    count = lax.axis_size(axis)
    route = []
    for low in range(count):
        high = low | 1 << bit
        if high != low and high < count:
            route += [(low, high), (high, low)]
    return lax.ppermute(block, axis, route)


def with_halo(cells, sides, width):
    for axis, dim in sides:
        count = lax.axis_size(axis)
        head = lax.slice_in_dim(cells, 0, width, axis=dim)
        tail = lax.slice_in_dim(cells, cells.shape[dim] - width, cells.shape[dim], axis=dim)
        cells = jnp.concatenate(
            [
                lax.ppermute(tail, axis, [(i, (i + 1) % count) for i in range(count)]),
                cells,
                lax.ppermute(head, axis, [((i + 1) % count, i) for i in range(count)]),
            ],
            axis=dim,
        )
    return cells


def fast_substep(height, east_flow, north_flow, depth_field, wet_inside, inside, pushes):
    flux_east = depth_field * east_flow
    flux_north = depth_field * north_flow
    west_flux = jnp.roll(flux_east, 1, axis=1)
    south_flux = jnp.roll(flux_north, 1, axis=0)
    height_next = inside * (
        height - STEP_SIZE * (flux_east - west_flux + (flux_north - south_flux)) + pushes[0]
    )
    east_height = jnp.roll(height_next, -1, axis=1)
    north_height = jnp.roll(height_next, -1, axis=0)
    east_next = wet_inside * (
        DAMPING * east_flow - STEP_SIZE * (east_height - height_next) + pushes[1]
    )
    north_next = wet_inside * (
        DAMPING * north_flow - STEP_SIZE * (north_height - height_next) + pushes[2]
    )
    return (height_next, east_next, north_next)


def body(
    column,
    fast_state,
    wave_depth,
    wet_mask,
    surface,
    coupling,
    emission,
    remap_weight,
    send_block,
    link_slot,
):
    wet_float = wet_mask[0].astype(jnp.float32)
    outgoing = (surface[0] * wet_float[None]).astype(jnp.bfloat16)
    payload = outgoing[:, send_block[0, 0]]
    crossed = swapped(payload, "comp", 0)
    arrived = lax.all_to_all(crossed, "col", split_axis=1, concat_axis=1, tiled=True)
    flattened = arrived.reshape(Q, -1, W)
    linked = flattened[:, link_slot[0, 0]].reshape(Q, H, K, W).astype(jnp.float32)
    band_weights = remap_weight[0].astype(jnp.float32)
    span_cells = band_weights.shape[2]
    forcing = jnp.zeros((Q, H, W), jnp.float32)
    for offset in range(span_cells):
        shifted = jnp.roll(linked, span_cells // 2 - offset, axis=3)
        forcing = forcing + jnp.sum(shifted * band_weights[:, :, offset][None], axis=2)
    driving = jnp.einsum("mq,qhw->mhw", coupling[0], forcing, precision=lax.Precision.HIGHEST)
    levels = column.shape[1]
    updated = column[0] + driving[:levels]
    per_substep = 1.0 / SUBSTEPS
    pushes = driving[levels:] * per_substep
    rim_cells = 1
    statics = jnp.concatenate([wave_depth[0][None], wet_float[None], pushes], 0)
    extended = with_halo(statics, (("row", 1), ("col", 2)), rim_cells)
    band_rows = lax.axis_size("row") * H
    global_rows = (
        lax.axis_index("row") * H + jnp.arange(H + 2 * rim_cells, dtype=jnp.int32) - rim_cells
    )
    inside = ((global_rows >= 0) & (global_rows < band_rows)).astype(jnp.float32)[:, None]
    depth_ext = extended[0]
    wet_inside = extended[1] * inside
    pushes_ext = extended[2:5]

    def crop(stacked):
        return stacked[:, rim_cells : rim_cells + H, rim_cells : rim_cells + W]

    def advance(turn, carried):
        fields, totals = carried
        widened = with_halo(fields, (("row", 1), ("col", 2)), rim_cells) * inside
        height, east_flow, north_flow = (widened[0], widened[1], widened[2])
        height, east_flow, north_flow = fast_substep(
            height, east_flow, north_flow, depth_ext, wet_inside, inside, pushes_ext
        )
        totals = totals + crop(jnp.stack([height, east_flow, north_flow]))
        return (crop(jnp.stack([height, east_flow, north_flow])), totals)

    start = (fast_state[0], jnp.zeros((3, H, W), jnp.float32))
    final_fields, totals = lax.fori_loop(0, SUBSTEPS // rim_cells, advance, start)
    stacked = jnp.concatenate([updated, totals * per_substep], 0)
    emitted = jnp.tanh(
        jnp.einsum("qm,mhw->qhw", emission[0], stacked, precision=lax.Precision.HIGHEST)
    )
    return (updated[None], final_fields[None], emitted[None])


def solution(mesh):
    placed = (
        P("comp", None, "row", "col"),
        P("comp", None, "row", "col"),
        P("comp", "row", "col"),
        P("comp", "row", "col"),
        P("comp", None, "row", "col"),
        P("comp", None, None),
        P("comp", None, None),
        P("comp", "row", "col", None, None),
        P("comp", "row", "col", None),
        P("comp", "row", "col"),
    )
    return jax.shard_map(
        body,
        mesh=mesh,
        in_specs=placed,
        out_specs=(
            P("comp", None, "row", "col"),
            P("comp", None, "row", "col"),
            P("comp", None, "row", "col"),
        ),
        check_vma=False,
    )
```

profile of v0, /device:TPU:0, one launch (start us, length us, event | category | flops | bytes accessed | tf_op | source)
XLA Modules:
  0.0 370.7 jit_solution(7335604038961238761)
XLA Ops:
  3.0 3.0 collective-permute-start.4
  6.1 6.4 %collective-permute-done.4 = bf16[8,4,32,128]{3,0,2,1:T(8,128)(2,1)} collective-permute-done((bf16[8,4,32,128]{3,0,2,1:T(8,128)(2,1)S(1)}, bf16[8,4,32,128]{3,0,2,1:T(8,128)(2,1)}, u32[]{:S(2)}, u32[]{:S(2)}) %collective-permute-start.4) | collective-permute-done | bytes 262176 | tf_op jit(solution)/shard_map/ppermute | solution.py:24
  12.4 3.4 all-to-all-start
  16.1 5.8 %all-to-all-done = bf16[8,4,32,128]{3,0,2,1:T(8,128)(2,1)S(1)} async-done(((bf16[8,4,32,128]{3,0,2,1:T(8,128)(2,1)}), bf16[8,4,32,128]{3,0,2,1:T(8,128)(2,1)S(1)}, u32[]{:S(2)}, u32[]{:S(2)}) %all-to-all-start) | async-done | bytes 262176 | tf_op jit(solution)/shard_map/all_to_all | solution.py:78
  26.9 2.1 collective-permute-start.6
  33.3 2.9 collective-permute-done.7
  37.9 331.0 %while.15 = (s32[]{:T(128)}, f32[3,32,128]{2,1,0:T(8,128)S(1)}, f32[3,32,128]{2,1,0:T(8,128)S(1)}, f32[34,130]{1,0:T(8,128)S(1)}, f32[3,34,130]{2,1,0:T(8,128)S(...) while((s32[]{:T(128)}, f32[3,32,128]{2,1,0:T(8,128)S(1)}, ...), condition=%wide.region_5.6_spmd.clone.clone.clone, body=%wide.region_4.5_spmd.clone.clone.clone.sunk | while | flops 301095 | bytes 1142503 | solution.py:118
  37.9 3.8 %collective-permute-start = (f32[3,1,128]{2,1,0:T(1,128)S(1)}, f32[3,1,128]{2,1,0:T(1,128)S(1)}, u32[]{:S(2)}, u32[]{:S(2)}) collective-permute-start(f32[3,1,128]{2,1,0:T(1,128)S(1)} %get-tuple-element.271), channel_id=1, source_target_pairs={{4,0},{8,4},{12,8},{0,12},{5,1},{9,5},{13,9},{1,13},{6,2},{10,6},{... | collective-permute-start | bytes 4616 | tf_op jit(solution)/shard_map/while/body/eval_jaxpr/ppermute | solution.py:36
  43.1 4.1 %collective-permute-done.1 = f32[3,1,128]{2,1,0:T(1,128)S(1)} collective-permute-done((f32[3,1,128]{2,1,0:T(1,128)S(1)}, f32[3,1,128]{2,1,0:T(1,128)S(1)}, u32[]{:S(2)}, u32[]{:S(2)}) %collective-permute-start.1) | collective-permute-done | bytes 1568 | tf_op jit(solution)/shard_map/while/body/eval_jaxpr/ppermute | solution.py:34
  59.2 2.2 collective-permute-done.3
  62.2 2.0 collective-permute-start.1
  72.2 2.0 collective-permute-start.1
  79.7 2.2 collective-permute-done.3
  100.1 2.2 collective-permute-done.3
  103.1 2.0 collective-permute-start.1
  113.2 2.0 collective-permute-start.1
  120.6 2.2 collective-permute-done.3
  141.0 2.2 collective-permute-done.3
  144.0 2.0 collective-permute-start.1
  154.1 2.0 collective-permute-start.1
  161.5 2.2 collective-permute-done.3
  164.5 2.0 collective-permute-start.1
  182.0 2.2 collective-permute-done.3
  202.4 2.2 collective-permute-done.3
  222.9 2.2 collective-permute-done.3
  243.3 2.2 collective-permute-done.3
  263.8 2.2 collective-permute-done.3
  284.2 2.2 collective-permute-done.3
  304.7 2.2 collective-permute-done.3
  325.2 2.2 collective-permute-done.3
  345.6 2.2 collective-permute-done.3
  366.1 2.2 collective-permute-done.3
  (898 shorter events, 285.8 us)
Async XLA Ops:
  3.0 9.4 %collective-permute-start.4 = (bf16[8,4,32,128]{3,0,2,1:T(8,128)(2,1)S(1)}, bf16[8,4,32,128]{3,0,2,1:T(8,128)(2,1)}, u32[]{:S(2)}, u32[]{:S(2)}) collective-permute-start(bf16[8,4,32,128]{3,0,2,1:T(8,128)(2,1)S(1)} %bitcast.130), channel_id=1, source_target_pairs={{0,16},{16,0},{1,17},{17,1},{2,18},{18,2},{3,19},{19,3},{4,20},{20... | collective-permute-start | bytes 786440 | tf_op jit(solution)/shard_map/ppermute | solution.py:24
  12.4 9.4 %all-to-all-start = ((bf16[8,4,32,128]{3,0,2,1:T(8,128)(2,1)}), bf16[8,4,32,128]{3,0,2,1:T(8,128)(2,1)S(1)}, u32[]{:S(2)}, u32[]{:S(2)}) async-start(bf16[8,4,32,128]{3,0,2,1:T(8,128)(2,1)} %collective-permute-done.4), calls=%async_computation | async-start | bytes 524288 | tf_op jit(solution)/shard_map/all_to_all | solution.py:78
  25.0 5.5 %collective-permute-start.5 = (f32[5,1,128]{2,0,1:T(8,128)S(1)}, f32[5,1,128]{2,0,1:T(8,128)S(1)}, u32[]{:S(2)}, u32[]{:S(2)}) collective-permute-start(f32[5,1,128]{2,0,1:T(8,128)S(1)} %get-tuple-element.204), channel_id=1, source_target_pairs={{0,4},{4,8},{8,12},{12,0},{1,5},{5,9},{9,13},{13,1},{2,6},{6,10},{... | collective-permute-start | bytes 7688 | tf_op jit(solution)/shard_map/ppermute | solution.py:34
  62.2 5.4 %collective-permute-start.1 = (f32[3,1,128]{2,1,0:T(1,128)S(1)}, f32[3,1,128]{2,1,0:T(1,128)S(1)}, u32[]{:S(2)}, u32[]{:S(2)}) collective-permute-start(f32[3,1,128]{2,1,0:T(1,128)S(1)} %get-tuple-element.272), channel_id=1, source_target_pairs={{0,4},{4,8},{8,12},{12,0},{1,5},{5,9},{9,13},{13,1},{2,6},{6,10},{... | collective-permute-start | bytes 4616 | tf_op jit(solution)/shard_map/while/body/eval_jaxpr/ppermute | solution.py:34
  72.2 5.4 %collective-permute-start.1 = (f32[3,1,128]{2,1,0:T(1,128)S(1)}, f32[3,1,128]{2,1,0:T(1,128)S(1)}, u32[]{:S(2)}, u32[]{:S(2)}) collective-permute-start(f32[3,1,128]{2,1,0:T(1,128)S(1)} %get-tuple-element.272), channel_id=1, source_target_pairs={{0,4},{4,8},{8,12},{12,0},{1,5},{5,9},{9,13},{13,1},{2,6},{6,10},{... | collective-permute-start | bytes 4616 | tf_op jit(solution)/shard_map/while/body/eval_jaxpr/ppermute | solution.py:34
  82.6 5.4 %collective-permute-start.1 = (f32[3,1,128]{2,1,0:T(1,128)S(1)}, f32[3,1,128]{2,1,0:T(1,128)S(1)}, u32[]{:S(2)}, u32[]{:S(2)}) collective-permute-start(f32[3,1,128]{2,1,0:T(1,128)S(1)} %get-tuple-element.272), channel_id=1, source_target_pairs={{0,4},{4,8},{8,12},{12,0},{1,5},{5,9},{9,13},{13,1},{2,6},{6,10},{... | collective-permute-start | bytes 4616 | tf_op jit(solution)/shard_map/while/body/eval_jaxpr/ppermute | solution.py:34
  92.7 5.4 %collective-permute-start.1 = (f32[3,1,128]{2,1,0:T(1,128)S(1)}, f32[3,1,128]{2,1,0:T(1,128)S(1)}, u32[]{:S(2)}, u32[]{:S(2)}) collective-permute-start(f32[3,1,128]{2,1,0:T(1,128)S(1)} %get-tuple-element.272), channel_id=1, source_target_pairs={{0,4},{4,8},{8,12},{12,0},{1,5},{5,9},{9,13},{13,1},{2,6},{6,10},{... | collective-permute-start | bytes 4616 | tf_op jit(solution)/shard_map/while/body/eval_jaxpr/ppermute | solution.py:34
  103.1 5.4 %collective-permute-start.1 = (f32[3,1,128]{2,1,0:T(1,128)S(1)}, f32[3,1,128]{2,1,0:T(1,128)S(1)}, u32[]{:S(2)}, u32[]{:S(2)}) collective-permute-start(f32[3,1,128]{2,1,0:T(1,128)S(1)} %get-tuple-element.272), channel_id=1, source_target_pairs={{0,4},{4,8},{8,12},{12,0},{1,5},{5,9},{9,13},{13,1},{2,6},{6,10},{... | collective-permute-start | bytes 4616 | tf_op jit(solution)/shard_map/while/body/eval_jaxpr/ppermute | solution.py:34
  113.2 5.4 %collective-permute-start.1 = (f32[3,1,128]{2,1,0:T(1,128)S(1)}, f32[3,1,128]{2,1,0:T(1,128)S(1)}, u32[]{:S(2)}, u32[]{:S(2)}) collective-permute-start(f32[3,1,128]{2,1,0:T(1,128)S(1)} %get-tuple-element.272), channel_id=1, source_target_pairs={{0,4},{4,8},{8,12},{12,0},{1,5},{5,9},{9,13},{13,1},{2,6},{6,10},{... | collective-permute-start | bytes 4616 | tf_op jit(solution)/shard_map/while/body/eval_jaxpr/ppermute | solution.py:34
  123.6 5.4 %collective-permute-start.1 = (f32[3,1,128]{2,1,0:T(1,128)S(1)}, f32[3,1,128]{2,1,0:T(1,128)S(1)}, u32[]{:S(2)}, u32[]{:S(2)}) collective-permute-start(f32[3,1,128]{2,1,0:T(1,128)S(1)} %get-tuple-element.272), channel_id=1, source_target_pairs={{0,4},{4,8},{8,12},{12,0},{1,5},{5,9},{9,13},{13,1},{2,6},{6,10},{... | collective-permute-start | bytes 4616 | tf_op jit(solution)/shard_map/while/body/eval_jaxpr/ppermute | solution.py:34
  133.6 5.4 %collective-permute-start.1 = (f32[3,1,128]{2,1,0:T(1,128)S(1)}, f32[3,1,128]{2,1,0:T(1,128)S(1)}, u32[]{:S(2)}, u32[]{:S(2)}) collective-permute-start(f32[3,1,128]{2,1,0:T(1,128)S(1)} %get-tuple-element.272), channel_id=1, source_target_pairs={{0,4},{4,8},{8,12},{12,0},{1,5},{5,9},{9,13},{13,1},{2,6},{6,10},{... | collective-permute-start | bytes 4616 | tf_op jit(solution)/shard_map/while/body/eval_jaxpr/ppermute | solution.py:34
  144.0 5.4 %collective-permute-start.1 = (f32[3,1,128]{2,1,0:T(1,128)S(1)}, f32[3,1,128]{2,1,0:T(1,128)S(1)}, u32[]{:S(2)}, u32[]{:S(2)}) collective-permute-start(f32[3,1,128]{2,1,0:T(1,128)S(1)} %get-tuple-element.272), channel_id=1, source_target_pairs={{0,4},{4,8},{8,12},{12,0},{1,5},{5,9},{9,13},{13,1},{2,6},{6,10},{... | collective-permute-start | bytes 4616 | tf_op jit(solution)/shard_map/while/body/eval_jaxpr/ppermute | solution.py:34
  154.1 5.4 %collective-permute-start.1 = (f32[3,1,128]{2,1,0:T(1,128)S(1)}, f32[3,1,128]{2,1,0:T(1,128)S(1)}, u32[]{:S(2)}, u32[]{:S(2)}) collective-permute-start(f32[3,1,128]{2,1,0:T(1,128)S(1)} %get-tuple-element.272), channel_id=1, source_target_pairs={{0,4},{4,8},{8,12},{12,0},{1,5},{5,9},{9,13},{13,1},{2,6},{6,10},{... | collective-permute-start | bytes 4616 | tf_op jit(solution)/shard_map/while/body/eval_jaxpr/ppermute | solution.py:34
  164.5 5.4 %collective-permute-start.1 = (f32[3,1,128]{2,1,0:T(1,128)S(1)}, f32[3,1,128]{2,1,0:T(1,128)S(1)}, u32[]{:S(2)}, u32[]{:S(2)}) collective-permute-start(f32[3,1,128]{2,1,0:T(1,128)S(1)} %get-tuple-element.272), channel_id=1, source_target_pairs={{0,4},{4,8},{8,12},{12,0},{1,5},{5,9},{9,13},{13,1},{2,6},{6,10},{... | collective-permute-start | bytes 4616 | tf_op jit(solution)/shard_map/while/body/eval_jaxpr/ppermute | solution.py:34
  174.5 5.4 %collective-permute-start.1 = (f32[3,1,128]{2,1,0:T(1,128)S(1)}, f32[3,1,128]{2,1,0:T(1,128)S(1)}, u32[]{:S(2)}, u32[]{:S(2)}) collective-permute-start(f32[3,1,128]{2,1,0:T(1,128)S(1)} %get-tuple-element.272), channel_id=1, source_target_pairs={{0,4},{4,8},{8,12},{12,0},{1,5},{5,9},{9,13},{13,1},{2,6},{6,10},{... | collective-permute-start | bytes 4616 | tf_op jit(solution)/shard_map/while/body/eval_jaxpr/ppermute | solution.py:34
  184.9 5.4 %collective-permute-start.1 = (f32[3,1,128]{2,1,0:T(1,128)S(1)}, f32[3,1,128]{2,1,0:T(1,128)S(1)}, u32[]{:S(2)}, u32[]{:S(2)}) collective-permute-start(f32[3,1,128]{2,1,0:T(1,128)S(1)} %get-tuple-element.272), channel_id=1, source_target_pairs={{0,4},{4,8},{8,12},{12,0},{1,5},{5,9},{9,13},{13,1},{2,6},{6,10},{... | collective-permute-start | bytes 4616 | tf_op jit(solution)/shard_map/while/body/eval_jaxpr/ppermute | solution.py:34
  195.0 5.4 %collective-permute-start.1 = (f32[3,1,128]{2,1,0:T(1,128)S(1)}, f32[3,1,128]{2,1,0:T(1,128)S(1)}, u32[]{:S(2)}, u32[]{:S(2)}) collective-permute-start(f32[3,1,128]{2,1,0:T(1,128)S(1)} %get-tuple-element.272), channel_id=1, source_target_pairs={{0,4},{4,8},{8,12},{12,0},{1,5},{5,9},{9,13},{13,1},{2,6},{6,10},{... | collective-permute-start | bytes 4616 | tf_op jit(solution)/shard_map/while/body/eval_jaxpr/ppermute | solution.py:34
  205.4 5.4 %collective-permute-start.1 = (f32[3,1,128]{2,1,0:T(1,128)S(1)}, f32[3,1,128]{2,1,0:T(1,128)S(1)}, u32[]{:S(2)}, u32[]{:S(2)}) collective-permute-start(f32[3,1,128]{2,1,0:T(1,128)S(1)} %get-tuple-element.272), channel_id=1, source_target_pairs={{0,4},{4,8},{8,12},{12,0},{1,5},{5,9},{9,13},{13,1},{2,6},{6,10},{... | collective-permute-start | bytes 4616 | tf_op jit(solution)/shard_map/while/body/eval_jaxpr/ppermute | solution.py:34
  215.4 5.4 %collective-permute-start.1 = (f32[3,1,128]{2,1,0:T(1,128)S(1)}, f32[3,1,128]{2,1,0:T(1,128)S(1)}, u32[]{:S(2)}, u32[]{:S(2)}) collective-permute-start(f32[3,1,128]{2,1,0:T(1,128)S(1)} %get-tuple-element.272), channel_id=1, source_target_pairs={{0,4},{4,8},{8,12},{12,0},{1,5},{5,9},{9,13},{13,1},{2,6},{6,10},{... | collective-permute-start | bytes 4616 | tf_op jit(solution)/shard_map/while/body/eval_jaxpr/ppermute | solution.py:34
  225.8 5.4 %collective-permute-start.1 = (f32[3,1,128]{2,1,0:T(1,128)S(1)}, f32[3,1,128]{2,1,0:T(1,128)S(1)}, u32[]{:S(2)}, u32[]{:S(2)}) collective-permute-start(f32[3,1,128]{2,1,0:T(1,128)S(1)} %get-tuple-element.272), channel_id=1, source_target_pairs={{0,4},{4,8},{8,12},{12,0},{1,5},{5,9},{9,13},{13,1},{2,6},{6,10},{... | collective-permute-start | bytes 4616 | tf_op jit(solution)/shard_map/while/body/eval_jaxpr/ppermute | solution.py:34
  235.9 5.4 %collective-permute-start.1 = (f32[3,1,128]{2,1,0:T(1,128)S(1)}, f32[3,1,128]{2,1,0:T(1,128)S(1)}, u32[]{:S(2)}, u32[]{:S(2)}) collective-permute-start(f32[3,1,128]{2,1,0:T(1,128)S(1)} %get-tuple-element.272), channel_id=1, source_target_pairs={{0,4},{4,8},{8,12},{12,0},{1,5},{5,9},{9,13},{13,1},{2,6},{6,10},{... | collective-permute-start | bytes 4616 | tf_op jit(solution)/shard_map/while/body/eval_jaxpr/ppermute | solution.py:34
  246.3 5.4 %collective-permute-start.1 = (f32[3,1,128]{2,1,0:T(1,128)S(1)}, f32[3,1,128]{2,1,0:T(1,128)S(1)}, u32[]{:S(2)}, u32[]{:S(2)}) collective-permute-start(f32[3,1,128]{2,1,0:T(1,128)S(1)} %get-tuple-element.272), channel_id=1, source_target_pairs={{0,4},{4,8},{8,12},{12,0},{1,5},{5,9},{9,13},{13,1},{2,6},{6,10},{... | collective-permute-start | bytes 4616 | tf_op jit(solution)/shard_map/while/body/eval_jaxpr/ppermute | solution.py:34
  256.4 5.4 %collective-permute-start.1 = (f32[3,1,128]{2,1,0:T(1,128)S(1)}, f32[3,1,128]{2,1,0:T(1,128)S(1)}, u32[]{:S(2)}, u32[]{:S(2)}) collective-permute-start(f32[3,1,128]{2,1,0:T(1,128)S(1)} %get-tuple-element.272), channel_id=1, source_target_pairs={{0,4},{4,8},{8,12},{12,0},{1,5},{5,9},{9,13},{13,1},{2,6},{6,10},{... | collective-permute-start | bytes 4616 | tf_op jit(solution)/shard_map/while/body/eval_jaxpr/ppermute | solution.py:34
  266.8 5.4 %collective-permute-start.1 = (f32[3,1,128]{2,1,0:T(1,128)S(1)}, f32[3,1,128]{2,1,0:T(1,128)S(1)}, u32[]{:S(2)}, u32[]{:S(2)}) collective-permute-start(f32[3,1,128]{2,1,0:T(1,128)S(1)} %get-tuple-element.272), channel_id=1, source_target_pairs={{0,4},{4,8},{8,12},{12,0},{1,5},{5,9},{9,13},{13,1},{2,6},{6,10},{... | collective-permute-start | bytes 4616 | tf_op jit(solution)/shard_map/while/body/eval_jaxpr/ppermute | solution.py:34
  276.8 5.4 %collective-permute-start.1 = (f32[3,1,128]{2,1,0:T(1,128)S(1)}, f32[3,1,128]{2,1,0:T(1,128)S(1)}, u32[]{:S(2)}, u32[]{:S(2)}) collective-permute-start(f32[3,1,128]{2,1,0:T(1,128)S(1)} %get-tuple-element.272), channel_id=1, source_target_pairs={{0,4},{4,8},{8,12},{12,0},{1,5},{5,9},{9,13},{13,1},{2,6},{6,10},{... | collective-permute-start | bytes 4616 | tf_op jit(solution)/shard_map/while/body/eval_jaxpr/ppermute | solution.py:34
  287.2 5.4 %collective-permute-start.1 = (f32[3,1,128]{2,1,0:T(1,128)S(1)}, f32[3,1,128]{2,1,0:T(1,128)S(1)}, u32[]{:S(2)}, u32[]{:S(2)}) collective-permute-start(f32[3,1,128]{2,1,0:T(1,128)S(1)} %get-tuple-element.272), channel_id=1, source_target_pairs={{0,4},{4,8},{8,12},{12,0},{1,5},{5,9},{9,13},{13,1},{2,6},{6,10},{... | collective-permute-start | bytes 4616 | tf_op jit(solution)/shard_map/while/body/eval_jaxpr/ppermute | solution.py:34
  297.3 5.4 %collective-permute-start.1 = (f32[3,1,128]{2,1,0:T(1,128)S(1)}, f32[3,1,128]{2,1,0:T(1,128)S(1)}, u32[]{:S(2)}, u32[]{:S(2)}) collective-permute-start(f32[3,1,128]{2,1,0:T(1,128)S(1)} %get-tuple-element.272), channel_id=1, source_target_pairs={{0,4},{4,8},{8,12},{12,0},{1,5},{5,9},{9,13},{13,1},{2,6},{6,10},{... | collective-permute-start | bytes 4616 | tf_op jit(solution)/shard_map/while/body/eval_jaxpr/ppermute | solution.py:34
  307.7 5.4 %collective-permute-start.1 = (f32[3,1,128]{2,1,0:T(1,128)S(1)}, f32[3,1,128]{2,1,0:T(1,128)S(1)}, u32[]{:S(2)}, u32[]{:S(2)}) collective-permute-start(f32[3,1,128]{2,1,0:T(1,128)S(1)} %get-tuple-element.272), channel_id=1, source_target_pairs={{0,4},{4,8},{8,12},{12,0},{1,5},{5,9},{9,13},{13,1},{2,6},{6,10},{... | collective-permute-start | bytes 4616 | tf_op jit(solution)/shard_map/while/body/eval_jaxpr/ppermute | solution.py:34
  317.7 5.4 %collective-permute-start.1 = (f32[3,1,128]{2,1,0:T(1,128)S(1)}, f32[3,1,128]{2,1,0:T(1,128)S(1)}, u32[]{:S(2)}, u32[]{:S(2)}) collective-permute-start(f32[3,1,128]{2,1,0:T(1,128)S(1)} %get-tuple-element.272), channel_id=1, source_target_pairs={{0,4},{4,8},{8,12},{12,0},{1,5},{5,9},{9,13},{13,1},{2,6},{6,10},{... | collective-permute-start | bytes 4616 | tf_op jit(solution)/shard_map/while/body/eval_jaxpr/ppermute | solution.py:34
  328.1 5.4 %collective-permute-start.1 = (f32[3,1,128]{2,1,0:T(1,128)S(1)}, f32[3,1,128]{2,1,0:T(1,128)S(1)}, u32[]{:S(2)}, u32[]{:S(2)}) collective-permute-start(f32[3,1,128]{2,1,0:T(1,128)S(1)} %get-tuple-element.272), channel_id=1, source_target_pairs={{0,4},{4,8},{8,12},{12,0},{1,5},{5,9},{9,13},{13,1},{2,6},{6,10},{... | collective-permute-start | bytes 4616 | tf_op jit(solution)/shard_map/while/body/eval_jaxpr/ppermute | solution.py:34
  338.2 5.4 %collective-permute-start.1 = (f32[3,1,128]{2,1,0:T(1,128)S(1)}, f32[3,1,128]{2,1,0:T(1,128)S(1)}, u32[]{:S(2)}, u32[]{:S(2)}) collective-permute-start(f32[3,1,128]{2,1,0:T(1,128)S(1)} %get-tuple-element.272), channel_id=1, source_target_pairs={{0,4},{4,8},{8,12},{12,0},{1,5},{5,9},{9,13},{13,1},{2,6},{6,10},{... | collective-permute-start | bytes 4616 | tf_op jit(solution)/shard_map/while/body/eval_jaxpr/ppermute | solution.py:34
  348.6 5.4 %collective-permute-start.1 = (f32[3,1,128]{2,1,0:T(1,128)S(1)}, f32[3,1,128]{2,1,0:T(1,128)S(1)}, u32[]{:S(2)}, u32[]{:S(2)}) collective-permute-start(f32[3,1,128]{2,1,0:T(1,128)S(1)} %get-tuple-element.272), channel_id=1, source_target_pairs={{0,4},{4,8},{8,12},{12,0},{1,5},{5,9},{9,13},{13,1},{2,6},{6,10},{... | collective-permute-start | bytes 4616 | tf_op jit(solution)/shard_map/while/body/eval_jaxpr/ppermute | solution.py:34
  (111 other events, 372.3 us)
where the time goes:
time: 371 us
  waiting for transfers between devices  235 us (63%)
  starting transfers between devices  97.1 us (26%)
  other arithmetic  18.7 us (5%)
  local copies, waits for them, and re-layouts  14.4 us (4%)
  loops' own time  3.95 us (1%)
    ppermute x66, waiting for transfers between devices, with_halo(): lax.ppermute(tail, axis, [(i, (i + 1) % count) for i in range(count)])  127 us
    ppermute x66, waiting for transfers between devices, with_halo(): lax.ppermute(head, axis, [((i + 1) % count, i) for i in range(count)])  95.9 us
    ppermute x66, starting transfers between devices, with_halo(): lax.ppermute(tail, axis, [(i, (i + 1) % count) for i in range(count)])  80.2 us
    ppermute x66, starting transfers between devices, with_halo(): lax.ppermute(head, axis, [((i + 1) % count, i) for i in range(count)])  10.5 us
  transfers between devices with their start and end apart: 134, of which 132 were waited for; matrix products, arithmetic and copies ran while one was open for 0% of the time, Pallas kernels for 0%

commit v1 on v0

v1 whole, which is shorter than its diff:
```python
import functools

import jax
import jax.numpy as jnp
from jax import lax
from jax.experimental import pallas as pl
from jax.experimental.pallas import tpu as pltpu
from jax.sharding import PartitionSpec as P

H = 32
W = 128
K = 4
SPAN = 4
Q = 8
L = 8
SUBSTEPS = 32
FAST = 3
STEP_SIZE = 0.35
DAMPING = 0.97
CHUNKS = 2
PART = 32
ROWS = 3 * H
MESH = pl.DeviceIdType.MESH
TURNS = [(dr, dc) for dr in (-1, 0, 1) for dc in (-1, 0, 1) if (dr, dc) != (0, 0)]


def table_rows(peers):
    return max(16, -(-peers // 16) * 16)


def mask_order(peers):
    bits = peers.bit_length() - 1
    return sorted(range(peers), key=lambda m: int(format(m, "b").zfill(bits)[::-1], 2))


def lower_bits(mask, peers):
    bits = [1 << b for b in reversed(range(peers.bit_length() - 1))]
    return [b for b in bits if mask == 0 or b < (mask & -mask)]


def kernel(
    peers,
    bands,
    column,
    fast_state,
    depth,
    wet_mask,
    surface,
    coupling,
    emission,
    weights,
    send_block,
    link_slot,
    new_column,
    fast_final,
    next_surface,
    mine,
    got,
    table,
    wide,
    turned,
    linked,
    forcing,
    field_a,
    field_e,
    field_w,
    edge_e,
    edge_w,
    push_a,
    push_e,
    push_w,
    pedge_e,
    pedge_w,
    wave,
    fixed,
    totals,
    block_send,
    block_recv,
    field_send,
    field_recv,
    push_send,
    push_recv,
):
    comp = lax.axis_index("comp")
    row = lax.axis_index("row")
    col = lax.axis_index("col")
    slots = send_block.shape[1]
    head = table_rows(peers)
    bits = peers.bit_length() - 1
    up_ok = row < bands - 1
    down_ok = row > 0

    def at(dr, dc):
        return {"row": row + dr, "col": lax.rem(col + dc + peers, peers)}

    def reaches(dr):
        return up_ok if dr > 0 else down_ok

    def guarded(dr, act):
        if dr == 0:
            act()
        else:
            pl.when(reaches(dr))(act)

    barrier = pltpu.get_barrier_semaphore()

    def greet(device):
        pl.semaphore_signal(barrier, inc=1, device_id=device, device_id_type=MESH)

    greet({"comp": 1 - comp})
    for b in range(bits):
        greet({"col": col ^ (1 << b)})
    for dr, dc in TURNS:
        guarded(dr, functools.partial(greet, at(dr, dc)))

    wet = wet_mask[...].astype(jnp.float32)
    table[...] = jnp.zeros_like(table)
    table[0:peers, 0:slots] = send_block[...].astype(jnp.float32)
    mine[0:head] = table[...].astype(jnp.bfloat16)
    for q in range(Q):
        mine[head + q * H : head + (q + 1) * H] = (surface[q] * wet).astype(jnp.bfloat16)

    lane = lax.broadcasted_iota(jnp.int32, (H, W), 1)

    def pack(fields, east, west, tile):
        low = jnp.zeros((H, W), jnp.float32)
        high = jnp.zeros((H, W), jnp.float32)
        for i, cells in enumerate(fields):
            here = (lane >= i * PART) & (lane < (i + 1) * PART)
            first = cells if i == 0 else pltpu.roll(cells, i * PART, 1)
            turn = (i * PART - (W - PART)) % W
            last = cells if turn == 0 else pltpu.roll(cells, turn, 1)
            low = jnp.where(here, first, low)
            high = jnp.where(here, last, high)
        west[tile] = low
        east[tile] = high

    own = slice(H, 2 * H)
    statics = [fast_state[i] for i in range(FAST)] + [depth[...], wet]
    for i, cells in enumerate(statics):
        field_a[i, own] = cells
    pack(statics[:4], edge_e, edge_w, 0)
    pack(statics[4:], edge_e, edge_w, 1)

    @pl.when(jnp.logical_not(down_ok))
    def _():
        for ref in (field_a, field_e, field_w, push_a, push_e, push_w):
            ref[:, 0:H] = jnp.zeros_like(ref[:, 0:H])

    @pl.when(jnp.logical_not(up_ok))
    def _():
        for ref in (field_a, field_e, field_w, push_a, push_e, push_w):
            ref[:, 2 * H : 3 * H] = jnp.zeros_like(ref[:, 2 * H : 3 * H])

    beyond = up_ok.astype(jnp.int32) + down_ok.astype(jnp.int32)
    pl.semaphore_wait(barrier, 1 + bits + 2 + 3 * beyond)

    chunk_rows = Q * H // CHUNKS

    def span_of(chunk):
        if chunk == 0:
            return pl.ds(0, head + chunk_rows)
        return pl.ds(head + chunk * chunk_rows, chunk_rows)

    def block_copy(mask, bit, chunk):
        source = col ^ mask
        index = (mask | bit) * CHUNKS + chunk
        return pltpu.make_async_remote_copy(
            src_ref=got.at[source, span_of(chunk)],
            dst_ref=got.at[source, span_of(chunk)],
            send_sem=block_send.at[index],
            recv_sem=block_recv.at[index],
            device_id={"col": col ^ bit},
            device_id_type=MESH,
        )

    def arrival(mask, chunk):
        source = col ^ mask
        index = mask * CHUNKS + chunk
        if mask == 0:
            return pltpu.make_async_remote_copy(
                src_ref=mine.at[span_of(chunk)],
                dst_ref=got.at[col, span_of(chunk)],
                send_sem=block_send.at[index],
                recv_sem=block_recv.at[index],
                device_id={"comp": 1 - comp},
                device_id_type=MESH,
            )
        bit = mask & -mask
        return pltpu.make_async_remote_copy(
            src_ref=got.at[source, span_of(chunk)],
            dst_ref=got.at[source, span_of(chunk)],
            send_sem=block_send.at[index],
            recv_sem=block_recv.at[index],
            device_id={"col": col ^ bit},
            device_id_type=MESH,
        )

    def halo_copy(dr, dc, middle, east, west, land_e, land_w, send, recv):
        index = TURNS.index((dr, dc))
        land = pl.ds(H - H * dr, H)
        if dc == 0:
            src, dst = middle.at[:, pl.ds(H, H)], middle.at[:, land]
        elif dc > 0:
            src, dst = east, land_w.at[:, land]
        else:
            src, dst = west, land_e.at[:, land]
        return pltpu.make_async_remote_copy(
            src_ref=src,
            dst_ref=dst,
            send_sem=send.at[index],
            recv_sem=recv.at[index],
            device_id=at(dr, dc),
            device_id_type=MESH,
        )

    field_halo = (field_a, edge_e, edge_w, field_e, field_w, field_send, field_recv)
    push_halo = (push_a, pedge_e, pedge_w, push_e, push_w, push_send, push_recv)

    def send_halo(halo):
        for dr, dc in TURNS:
            guarded(dr, lambda dr=dr, dc=dc: halo_copy(dr, dc, *halo).start())

    def await_halo(halo):
        for dr, dc in TURNS:
            guarded(-dr, lambda dr=dr, dc=dc: halo_copy(dr, dc, *halo).wait_recv())

    def drain_halo(halo):
        for dr, dc in TURNS:
            guarded(dr, lambda dr=dr, dc=dc: halo_copy(dr, dc, *halo).wait_send())

    for chunk in range(CHUNKS):
        arrival(0, chunk).start()
    send_halo(field_halo)

    wide[...] = weights[...].astype(jnp.float32)
    for k in range(K):
        for d in range(SPAN):
            plane = wide[pl.ds(k * SPAN + d, H, stride=K * SPAN), :]
            turn = (d - SPAN // 2) % W
            turned[k * SPAN + d] = plane if turn == 0 else pltpu.roll(plane, turn, 1)

    links = H * K
    rows_l = lax.broadcasted_iota(jnp.int32, (links, links), 0)
    lanes_l = lax.broadcasted_iota(jnp.int32, (links, links), 1)

    def hot(condition):
        return jnp.where(condition, 1.0, 0.0).astype(jnp.bfloat16)

    def dot_nt(a, b):
        return lax.dot_general(
            a, b, (((1,), (1,)), ((), ())), preferred_element_type=jnp.float32
        )

    order = hot(lanes_l == (rows_l & (H - 1)) * K + (rows_l >> 5))
    by_slot = hot(rows_l == link_slot[...])
    slot_of_link = dot_nt(order, by_slot).astype(jnp.bfloat16)

    waited = []
    order_of = mask_order(peers)
    senders = [m for m in order_of if m == 0 or lower_bits(m, peers)]
    leaves = [m for m in order_of if m not in senders]

    def receive(mask, chunk):
        arrival(mask, chunk).wait_recv()
        for bit in lower_bits(mask, peers):
            block_copy(mask, bit, chunk).start()

    for mask in senders:
        for chunk in range(CHUNKS):
            receive(mask, chunk)
    pick = None
    per_chunk = Q // CHUNKS
    for chunk in range(CHUNKS):
        for mask in leaves:
            receive(mask, chunk)
        if chunk == 0:
            pieces = []
            rows_h = lax.broadcasted_iota(jnp.int32, (H, W), 0)
            rows_t = lax.broadcasted_iota(jnp.int32, (head, W), 0)
            for s in range(peers):
                listed = got[s, 0:head].astype(jnp.float32)
                chosen = jnp.sum(jnp.where(rows_t == col, listed, 0.0), axis=0, keepdims=True)
                chosen = jnp.broadcast_to(chosen, (H, W)).astype(jnp.int32)
                turn = s * slots % W
                chosen = chosen if turn == 0 else pltpu.roll(chosen, turn, 1)
                here = (lane >= s * slots) & (lane < (s + 1) * slots)
                pieces.append(hot(here & (chosen == rows_h)))
            block_of_slot = jnp.concatenate(pieces, axis=0)
            pick = dot_nt(slot_of_link, block_of_slot).astype(jnp.bfloat16)
        for pair in range(per_chunk // 2):
            first = chunk * per_chunk + 2 * pair
            cells = []
            for q in (first, first + 1):
                tall = got[:, head + q * H : head + (q + 1) * H, :]
                cells.append(tall.reshape(peers * H, W))
            linked[...] = jnp.dot(
                pick, jnp.concatenate(cells, axis=1), preferred_element_type=jnp.float32
            )
            for side in range(2):
                total = jnp.zeros((H, W), jnp.float32)
                for d in range(SPAN):
                    part = jnp.zeros((H, W), jnp.float32)
                    for k in range(K):
                        part = part + (
                            linked[k * H : (k + 1) * H, side * W : (side + 1) * W]
                            * turned[k * SPAN + d]
                        )
                    turn = (SPAN // 2 - d) % W
                    total = total + (part if turn == 0 else pltpu.roll(part, turn, 1))
                forcing[first + side] = total

    def driven(m, rows):
        total = coupling[0, m] * forcing[0, rows]
        for q in range(1, Q):
            total = total + coupling[q, m] * forcing[q, rows]
        return total

    everywhere = slice(0, H)
    pushes = [driven(L + i, everywhere) * (1.0 / SUBSTEPS) for i in range(FAST)]
    for i in range(FAST):
        push_a[i, own] = pushes[i]
    pack(pushes, pedge_e, pedge_w, 0)
    send_halo(push_halo)

    for m in range(L):
        new_column[m] = column[m] + driven(m, everywhere)
    for q in range(Q):
        total = emission[q, 0] * new_column[0]
        for m in range(1, L):
            total = total + emission[q, m] * new_column[m]
        next_surface[q] = total
    await_halo(field_halo)

    lane_r = lax.broadcasted_iota(jnp.int32, (ROWS, W), 1)

    def beside(east, west, i):
        tile, place = divmod(i, W // PART)
        near = east[tile]
        near = near if place == 0 else pltpu.roll(near, (W - place * PART) % W, 1)
        turn = (W - PART - place * PART) % W
        far = west[tile]
        far = far if turn == 0 else pltpu.roll(far, turn, 1)
        cells = jnp.where(lane_r < PART, near, 0.0)
        return jnp.where(lane_r >= W - PART, far, cells)

    scale = [STEP_SIZE, 1.0, 1.0, STEP_SIZE * STEP_SIZE, 1.0]
    for i in range(5):
        ref = wave.at[i] if i < FAST else fixed.at[i - FAST]
        ref[0] = field_a[i] * scale[i]
        ref[1] = beside(field_e, field_w, i) * scale[i]
    totals[...] = jnp.zeros_like(totals)
    await_halo(push_halo)
    pscale = [STEP_SIZE, 1.0, 1.0]
    for i in range(FAST):
        fixed[2 + i, 0] = push_a[i] * pscale[i]
        fixed[2 + i, 1] = beside(push_e, push_w, i) * pscale[i]

    lane8 = lax.broadcasted_iota(jnp.int32, (8, W), 1)
    sub8 = lax.broadcasted_iota(jnp.int32, (8, W), 0)
    west_rim = lane8 == 0
    east_rim = lane8 == W - 1
    south_rim = sub8 == 0
    north_rim = sub8 == 7
    top = jnp.where(up_ok, 1.0, 0.0).astype(jnp.float32)

    def sweep(low, high):
        south_prev = [jnp.zeros((8, W), jnp.float32)] * 2
        held = None
        for block in range(low, high + 2):
            rows = slice(8 * block, 8 * block + 8)
            now = None
            if block <= high:
                flow_e = [wave[1, t, rows] for t in range(2)]
                flow_n = [wave[2, t, rows] for t in range(2)]
                deep = [fixed[0, t, rows] for t in range(2)]
                flux_e = [deep[t] * flow_e[t] for t in range(2)]
                flux_n = [deep[t] * flow_n[t] for t in range(2)]
                spun = [pltpu.roll(flux_e[t], 1, 0 + 1) for t in range(2)]
                lifted = [pltpu.roll(flux_n[t], 1, 0) for t in range(2)]
                high_new = []
                for t in range(2):
                    from_west = jnp.where(west_rim, spun[1 - t], spun[t])
                    from_south = jnp.where(south_rim, south_prev[t], lifted[t])
                    level = (
                        wave[0, t, rows]
                        - ((flux_e[t] - from_west) + (flux_n[t] - from_south))
                        + fixed[2, t, rows]
                    )
                    if block == 2 * H // 8:
                        level = level * top
                    wave[0, t, rows] = level
                    high_new.append(level)
                if 4 <= block < 8:
                    orows = slice(8 * block - H, 8 * block - H + 8)
                    totals[0, orows] += high_new[0]
                south_prev = lifted
                down = [pltpu.roll(high_new[t], 7, 0) for t in range(2)]
                now = (rows, block, high_new, flow_e, flow_n, down)
            if held is not None:
                rows, block_h, level, flow_e, flow_n, down = held
                spun = [pltpu.roll(level[t], W - 1, 1) for t in range(2)]
                for t in range(2):
                    to_east = jnp.where(east_rim, spun[1 - t], spun[t])
                    if now is None:
                        to_north = down[t]
                    else:
                        to_north = jnp.where(north_rim, now[5][t], down[t])
                    open_cells = fixed[1, t, rows]
                    east = open_cells * (
                        DAMPING * flow_e[t] - (to_east - level[t]) + fixed[3, t, rows]
                    )
                    north = open_cells * (
                        DAMPING * flow_n[t] - (to_north - level[t]) + fixed[4, t, rows]
                    )
                    wave[1, t, rows] = east
                    wave[2, t, rows] = north
                    if t == 0 and 4 <= block_h < 8:
                        orows = slice(8 * block_h - H, 8 * block_h - H + 8)
                        totals[1, orows] += east
                        totals[2, orows] += north
            held = now

    for group in range(SUBSTEPS // 8):

        def step(_, carry, group=group):
            sweep(group, ROWS // 8 - 1 - group)
            return carry

        lax.fori_loop(0, 8, step, 0)

    back = [1.0 / STEP_SIZE, 1.0, 1.0]
    for i in range(FAST):
        fast_final[i] = wave[i, 0, own] * back[i]
    mean = [totals[i] * (back[i] / SUBSTEPS) for i in range(FAST)]
    for q in range(Q):
        total = next_surface[q]
        for i in range(FAST):
            total = total + emission[q, L + i] * mean[i]
        next_surface[q] = jnp.tanh(total)

    for chunk in range(CHUNKS):
        for mask in range(peers):
            arrival(mask, chunk).wait_send()
    drain_halo(field_halo)
    drain_halo(push_halo)


def solution(mesh):
    peers = mesh.shape["col"]
    bands = mesh.shape["row"]
    head = table_rows(peers)

    def body(
        column,
        fast_state,
        wave_depth,
        wet_mask,
        surface,
        coupling,
        emission,
        remap_weight,
        send_block,
        link_slot,
    ):
        f32 = jnp.float32
        vmem = pl.BlockSpec(memory_space=pltpu.VMEM)
        smem = pl.BlockSpec(memory_space=pltpu.SMEM)
        dma = pltpu.SemaphoreType.DMA
        outs = pl.pallas_call(
            functools.partial(kernel, peers, bands),
            out_shape=(
                jax.ShapeDtypeStruct((L, H, W), f32),
                jax.ShapeDtypeStruct((FAST, H, W), f32),
                jax.ShapeDtypeStruct((Q, H, W), f32),
            ),
            in_specs=[vmem] * 5 + [smem] * 2 + [vmem] * 3,
            out_specs=(vmem, vmem, vmem),
            scratch_shapes=[
                pltpu.VMEM((head + Q * H, W), jnp.bfloat16),
                pltpu.VMEM((peers, head + Q * H, W), jnp.bfloat16),
                pltpu.VMEM((head, W), f32),
                pltpu.VMEM((H * K * SPAN, W), f32),
                pltpu.VMEM((K * SPAN, H, W), f32),
                pltpu.VMEM((H * K, 2 * W), f32),
                pltpu.VMEM((Q, H, W), f32),
                pltpu.VMEM((5, ROWS, W), f32),
                pltpu.VMEM((2, ROWS, W), f32),
                pltpu.VMEM((2, ROWS, W), f32),
                pltpu.VMEM((2, H, W), f32),
                pltpu.VMEM((2, H, W), f32),
                pltpu.VMEM((FAST, ROWS, W), f32),
                pltpu.VMEM((1, ROWS, W), f32),
                pltpu.VMEM((1, ROWS, W), f32),
                pltpu.VMEM((1, H, W), f32),
                pltpu.VMEM((1, H, W), f32),
                pltpu.VMEM((FAST, 2, ROWS, W), f32),
                pltpu.VMEM((5, 2, ROWS, W), f32),
                pltpu.VMEM((FAST, H, W), f32),
                dma((peers * CHUNKS,)),
                dma((peers * CHUNKS,)),
                dma((8,)),
                dma((8,)),
                dma((8,)),
                dma((8,)),
            ],
            compiler_params=pltpu.CompilerParams(
                collective_id=0, has_side_effects=True, vmem_limit_bytes=40 << 20
            ),
        )(
            column[0],
            fast_state[0],
            wave_depth[0],
            wet_mask[0],
            surface[0],
            coupling[0].T,
            emission[0],
            remap_weight.reshape(H * K * SPAN, W),
            send_block[0, 0],
            link_slot[0],
        )
        return tuple(out[None] for out in outs)

    placed = (
        P("comp", None, "row", "col"),
        P("comp", None, "row", "col"),
        P("comp", "row", "col"),
        P("comp", "row", "col"),
        P("comp", None, "row", "col"),
        P("comp", None, None),
        P("comp", None, None),
        P("comp", "row", "col", None, None),
        P("comp", "row", "col", None),
        P("comp", "row", "col"),
    )
    return jax.shard_map(
        body,
        mesh=mesh,
        in_specs=placed,
        out_specs=(
            P("comp", None, "row", "col"),
            P("comp", None, "row", "col"),
            P("comp", None, "row", "col"),
        ),
        check_vma=False,
    )
```

time: 371 us -> 33.4 us (0.09)
  waiting for transfers between devices: 235 us -> 0 us
  starting transfers between devices: 97.1 us -> 0 us
  Pallas kernels: 0 us -> 24.1 us
  other arithmetic: 18.7 us -> 0 us
  local copies, waits for them, and re-layouts: 14.4 us -> 8.23 us
  loops' own time: 3.95 us -> 0 us
    ppermute x133 -> x0, waiting for transfers between devices: 229 us -> none  [the longest x66 127 us: with_halo(): lax.ppermute(tail, axis, [(i, (i + 1) % count) for i in range(count)])]
    ppermute x133 -> x0, starting transfers between devices: 93.7 us -> none  [the longest x66 80.2 us: with_halo(): lax.ppermute(tail, axis, [(i, (i + 1) % count) for i in range(count)])]
    pallas_call x0 -> x1, Pallas kernels: none -> 24.1 us  [body(): pl.pallas_call(functools.partial(kernel, peers, bands), out_shape=(jax.Sh...]
    mul x195 -> x0, other arithmetic: 11.9 us -> none  [the longest x32 4.19 us: advance(): widened = with_halo(fields, (('row', 1), ('col', 2)), rim_cells) * inside]
    all_to_all x1 -> x0, waiting for transfers between devices: 5.81 us -> none  [body(): lax.all_to_all(crossed, 'col', split_axis=1, concat_axis=1, tiled=True)]
    concatenate x256 -> x0, local copies, waits for them, and re-layouts: 5.79 us -> none  [the longest x64 2.56 us: fast_substep(): west_flux = jnp.roll(flux_east, 1, axis=1)]
    unnamed x22 -> x23, local copies, waits for them, and re-layouts: 3.48 us -> 8.23 us
    another operation x1 -> x0, loops' own time: 3.95 us -> none  [body(): lax.fori_loop(0, SUBSTEPS // rim_cells, advance, start)]
  transfers between devices with their start and end apart: 134 -> 0, of which waited for: 132 -> 0; matrix products, arithmetic and copies ran while one was open for 0% -> 0% of each run, Pallas kernels for 0% -> 0%
where the time goes in v1:
time: 33.4 us; the launch traced here: 33 us
  Pallas kernels  24.1 us (72%)
  local copies, waits for them, and re-layouts  8.23 us (25%)
  between operations  0.68 us (2%)
    pallas_call x1, Pallas kernels, body(): pl.pallas_call(functools.partial(kernel, peers, bands), out_shape=(jax.Sh...  24.1 us
    unnamed x23, local copies, waits for them, and re-layouts  8.23 us

profile of v1, /device:TPU:0, one launch (start us, length us, event | category | flops | bytes accessed | tf_op | source)
XLA Modules:
  0.0 33.0 jit_solution(3285184740159399433)
XLA Ops:
  0.6 0.0 copy-start.4
  0.6 0.0 copy-start.8
  0.7 0.0 copy-start.9
  0.7 0.7 %copy-done.4 = f32[1,32,128]{2,1,0:T(8,128)S(1)} copy-done((f32[1,32,128]{2,1,0:T(8,128)S(1)}, f32[1,32,128]{2,1,0:T(8,128)}, u32[]{:S(2)}) %copy-start.4) | copy-done | bytes 16408
  1.4 0.0 copy-done.8
  1.4 0.0 copy-done.9
  1.4 0.0 copy-start
  1.4 0.9 %copy-done = f32[1,8,32,128]{3,2,1,0:T(8,128)S(1)} copy-done((f32[1,8,32,128]{3,2,1,0:T(8,128)S(1)}, f32[1,8,32,128]{3,2,1,0:T(8,128)}, u32[]{:S(2)}) %copy-start) | copy-done | bytes 131096
  2.3 0.0 copy-start.1
  2.3 0.9 %copy-done.1 = f32[1,8,32,128]{3,2,1,0:T(8,128)S(1)} copy-done((f32[1,8,32,128]{3,2,1,0:T(8,128)S(1)}, f32[1,8,32,128]{3,2,1,0:T(8,128)}, u32[]{:S(2)}) %copy-start.1) | copy-done | bytes 131096
  3.2 0.0 copy-start.2
  3.2 0.9 %copy-done.2 = bf16[1,32,4,4,128]{4,3,2,1,0:T(4,128)(2,1)S(1)} copy-done((bf16[1,32,4,4,128]{4,3,2,1,0:T(4,128)(2,1)S(1)}, bf16[1,32,4,4,128]{4,3,2,1,0:T(4,128)(2,1)}, u32[]{:S(2)}) %copy-start.2) | copy-done | bytes 131096
  4.1 0.0 copy-start.3
  4.1 0.8 %copy-done.3 = f32[1,3,32,128]{3,2,1,0:T(8,128)S(1)} copy-done((f32[1,3,32,128]{3,2,1,0:T(8,128)S(1)}, f32[1,3,32,128]{3,2,1,0:T(8,128)}, u32[]{:S(2)}) %copy-start.3) | copy-done | bytes 49176
  4.9 0.0 copy-start.5
  4.9 0.7 %copy-done.5 = s32[1,32,128]{2,1,0:T(8,128)S(1)} copy-done((s32[1,32,128]{2,1,0:T(8,128)S(1)}, s32[1,32,128]{2,1,0:T(8,128)}, u32[]{:S(2)}) %copy-start.5) | copy-done | bytes 16408
  5.6 0.0 copy-start.6
  5.6 0.7 %copy-done.6 = f32[1,11,8]{1,2,0:T(8,128)S(1)} copy-done((f32[1,11,8]{1,2,0:T(8,128)S(1)}, f32[1,11,8]{1,2,0:T(8,128)}, u32[]{:S(2)}) %copy-start.6) | copy-done | bytes 376
  6.3 0.0 copy-start.7
  6.3 0.7 %copy-done.7 = f32[1,8,11]{2,1,0:T(8,128)S(1)} copy-done((f32[1,8,11]{2,1,0:T(8,128)S(1)}, f32[1,8,11]{2,1,0:T(8,128)}, u32[]{:S(2)}) %copy-start.7) | copy-done | bytes 376
  7.0 24.1 %shard_map.121 = (f32[8,32,128]{2,1,0:T(8,128)S(1)}, f32[3,32,128]{2,1,0:T(8,128)S(1)}, f32[8,32,128]{2,1,0:T(8,128)S(1)}) custom-call(f32[8,32,128]{2,1,0:T(8,128)S(1)} %bitcast.15, f32[3,32,128]{2,1,0:T(8,128)S(1)} %bitcast.20, f32[32,128]{1,0:T(8,128)S(1)} %bitcast.22, s32[32,128]{1,0:T(8,128)S(1)} %bitcast.23, f32[8,32,128]{2,1,0:T(8,128)S(1)} %bitcast.16, ...), custom_call_target="tpu_custom_call" | custom-call | tf_op jit(solution)/shard_map/pallas_call | solution.py:470
  31.0 0.7 %copy.16 = f32[1,8,32,128]{3,2,1,0:T(8,128)} copy(f32[1,8,32,128]{3,2,1,0:T(8,128)S(1)} %bitcast.19) | data formatting | bytes 262144
  31.7 0.6 %copy.17 = f32[1,3,32,128]{3,2,1,0:T(8,128)} copy(f32[1,3,32,128]{3,2,1,0:T(8,128)S(1)} %bitcast.21) | data formatting | bytes 98304
  32.3 0.7 %copy.18 = f32[1,8,32,128]{3,2,1,0:T(8,128)} copy(f32[1,8,32,128]{3,2,1,0:T(8,128)S(1)} %bitcast.18) | data formatting | bytes 262144
Async XLA Ops:
  0.6 0.7 %copy-start.4 = (f32[1,32,128]{2,1,0:T(8,128)S(1)}, f32[1,32,128]{2,1,0:T(8,128)}, u32[]{:S(2)}) copy-start(f32[1,32,128]{2,1,0:T(8,128)} %param.12) | copy-start | bytes 49156
  0.6 0.7 %copy-start.8 = (s32[1,1,4,32]{3,2,1,0:T(4,128)S(1)}, s32[1,1,4,32]{3,2,1,0:T(4,128)}, u32[]{:S(2)}) copy-start(s32[1,1,4,32]{3,2,1,0:T(4,128)} %param.18) | copy-start | bytes 1540
  0.7 0.7 %copy-start.9 = (s32[1,1,128]{2,1,0:T(1,128)S(1)}, s32[1,1,128]{2,1,0:T(1,128)}, u32[]{:S(2)}) copy-start(s32[1,1,128]{2,1,0:T(1,128)} %param.19) | copy-start | bytes 1540
  1.4 0.9 %copy-start = (f32[1,8,32,128]{3,2,1,0:T(8,128)S(1)}, f32[1,8,32,128]{3,2,1,0:T(8,128)}, u32[]{:S(2)}) copy-start(f32[1,8,32,128]{3,2,1,0:T(8,128)} %param.10) | copy-start | bytes 393220
  2.3 0.9 %copy-start.1 = (f32[1,8,32,128]{3,2,1,0:T(8,128)S(1)}, f32[1,8,32,128]{3,2,1,0:T(8,128)}, u32[]{:S(2)}) copy-start(f32[1,8,32,128]{3,2,1,0:T(8,128)} %param.14) | copy-start | bytes 393220
  3.2 0.9 %copy-start.2 = (bf16[1,32,4,4,128]{4,3,2,1,0:T(4,128)(2,1)S(1)}, bf16[1,32,4,4,128]{4,3,2,1,0:T(4,128)(2,1)}, u32[]{:S(2)}) copy-start(bf16[1,32,4,4,128]{4,3,2,1,0:T(4,128)(2,1)} %param.17) | copy-start | bytes 393220
  4.1 0.8 %copy-start.3 = (f32[1,3,32,128]{3,2,1,0:T(8,128)S(1)}, f32[1,3,32,128]{3,2,1,0:T(8,128)}, u32[]{:S(2)}) copy-start(f32[1,3,32,128]{3,2,1,0:T(8,128)} %param.11) | copy-start | bytes 147460
  4.9 0.7 %copy-start.5 = (s32[1,32,128]{2,1,0:T(8,128)S(1)}, s32[1,32,128]{2,1,0:T(8,128)}, u32[]{:S(2)}) copy-start(s32[1,32,128]{2,1,0:T(8,128)} %param.13) | copy-start | bytes 49156
  5.6 0.7 %copy-start.6 = (f32[1,11,8]{1,2,0:T(8,128)S(1)}, f32[1,11,8]{1,2,0:T(8,128)}, u32[]{:S(2)}) copy-start(f32[1,11,8]{1,2,0:T(8,128)} %param.15) | copy-start | bytes 1060
  6.3 0.7 %copy-start.7 = (f32[1,8,11]{2,1,0:T(8,128)S(1)}, f32[1,8,11]{2,1,0:T(8,128)}, u32[]{:S(2)}) copy-start(f32[1,8,11]{2,1,0:T(8,128)} %param.16) | copy-start | bytes 1060

commit v2 on v1

--- a/solution.py
+++ b/solution.py
@@ -38,9 +38,18 @@
     return [b for b in bits if mask == 0 or b < (mask & -mask)]
 
 
-def kernel(
+def kernel(peers, bands, *refs):
+    remap_kernel(peers, bands, refs[:10], *refs[10:])
+
+
+def remap_kernel(
     peers,
     bands,
+    sources,
+    new_column,
+    partial,
+    wave,
+    fixed,
     column,
     fast_state,
     depth,
@@ -51,9 +60,6 @@
     weights,
     send_block,
     link_slot,
-    new_column,
-    fast_final,
-    next_surface,
     mine,
     got,
     table,
@@ -71,9 +77,7 @@
     push_w,
     pedge_e,
     pedge_w,
-    wave,
-    fixed,
-    totals,
+    loaded,
     block_send,
     block_recv,
     field_send,
@@ -102,6 +106,25 @@
         else:
             pl.when(reaches(dr))(act)
 
+    held = (
+        column,
+        fast_state,
+        depth,
+        wet_mask,
+        surface,
+        coupling,
+        emission,
+        weights,
+        send_block,
+        link_slot,
+    )
+
+    def load(i):
+        return pltpu.make_async_copy(sources[i], held[i], loaded.at[i])
+
+    for i in (4, 3, 8, 1, 2, 7, 9, 5, 0, 6):
+        load(i).start()
+
     barrier = pltpu.get_barrier_semaphore()
 
     def greet(device):
@@ -113,44 +136,14 @@
     for dr, dc in TURNS:
         guarded(dr, functools.partial(greet, at(dr, dc)))
 
+    for i in (8, 3, 4):
+        load(i).wait()
     wet = wet_mask[...].astype(jnp.float32)
     table[...] = jnp.zeros_like(table)
     table[0:peers, 0:slots] = send_block[...].astype(jnp.float32)
     mine[0:head] = table[...].astype(jnp.bfloat16)
     for q in range(Q):
         mine[head + q * H : head + (q + 1) * H] = (surface[q] * wet).astype(jnp.bfloat16)
-
-    lane = lax.broadcasted_iota(jnp.int32, (H, W), 1)
-
-    def pack(fields, east, west, tile):
-        low = jnp.zeros((H, W), jnp.float32)
-        high = jnp.zeros((H, W), jnp.float32)
-        for i, cells in enumerate(fields):
-            here = (lane >= i * PART) & (lane < (i + 1) * PART)
-            first = cells if i == 0 else pltpu.roll(cells, i * PART, 1)
-            turn = (i * PART - (W - PART)) % W
-            last = cells if turn == 0 else pltpu.roll(cells, turn, 1)
-            low = jnp.where(here, first, low)
-            high = jnp.where(here, last, high)
-        west[tile] = low
-        east[tile] = high
-
-    own = slice(H, 2 * H)
-    statics = [fast_state[i] for i in range(FAST)] + [depth[...], wet]
-    for i, cells in enumerate(statics):
-        field_a[i, own] = cells
-    pack(statics[:4], edge_e, edge_w, 0)
-    pack(statics[4:], edge_e, edge_w, 1)
-
-    @pl.when(jnp.logical_not(down_ok))
-    def _():
-        for ref in (field_a, field_e, field_w, push_a, push_e, push_w):
-            ref[:, 0:H] = jnp.zeros_like(ref[:, 0:H])
-
-    @pl.when(jnp.logical_not(up_ok))
-    def _():
-        for ref in (field_a, field_e, field_w, push_a, push_e, push_w):
-            ref[:, 2 * H : 3 * H] = jnp.zeros_like(ref[:, 2 * H : 3 * H])
 
     beyond = up_ok.astype(jnp.int32) + down_ok.astype(jnp.int32)
     pl.semaphore_wait(barrier, 1 + bits + 2 + 3 * beyond)
@@ -231,8 +224,44 @@
 
     for chunk in range(CHUNKS):
         arrival(0, chunk).start()
+
+    lane = lax.broadcasted_iota(jnp.int32, (H, W), 1)
+
+    def pack(fields, east, west, tile):
+        low = jnp.zeros((H, W), jnp.float32)
+        high = jnp.zeros((H, W), jnp.float32)
+        for i, cells in enumerate(fields):
+            here = (lane >= i * PART) & (lane < (i + 1) * PART)
+            first = cells if i == 0 else pltpu.roll(cells, i * PART, 1)
+            turn = (i * PART - (W - PART)) % W
+            last = cells if turn == 0 else pltpu.roll(cells, turn, 1)
+            low = jnp.where(here, first, low)
+            high = jnp.where(here, last, high)
+        west[tile] = low
+        east[tile] = high
+
+    own = slice(H, 2 * H)
+    for i in (1, 2):
+        load(i).wait()
+    statics = [fast_state[i] for i in range(FAST)] + [depth[...], wet]
+    for i, cells in enumerate(statics):
+        field_a[i, own] = cells
+    pack(statics[:4], edge_e, edge_w, 0)
+    pack(statics[4:], edge_e, edge_w, 1)
+
+    @pl.when(jnp.logical_not(down_ok))
+    def _():
+        for ref in (field_a, field_e, field_w, push_a, push_e, push_w):
+            ref[:, 0:H] = jnp.zeros_like(ref[:, 0:H])
+
+    @pl.when(jnp.logical_not(up_ok))
+    def _():
+        for ref in (field_a, field_e, field_w, push_a, push_e, push_w):
+            ref[:, 2 * H : 3 * H] = jnp.zeros_like(ref[:, 2 * H : 3 * H])
+
     send_halo(field_halo)
 
+    load(7).wait()
     wide[...] = weights[...].astype(jnp.float32)
     for k in range(K):
         for d in range(SPAN):
@@ -252,6 +281,7 @@
             a, b, (((1,), (1,)), ((), ())), preferred_element_type=jnp.float32
         )
 
+    load(9).wait()
     order = hot(lanes_l == (rows_l & (H - 1)) * K + (rows_l >> 5))
     by_slot = hot(rows_l == link_slot[...])
     slot_of_link = dot_nt(order, by_slot).astype(jnp.bfloat16)
@@ -310,6 +340,8 @@
                     total = total + (part if turn == 0 else pltpu.roll(part, turn, 1))
                 forcing[first + side] = total
 
+    load(5).wait()
+
     def driven(m, rows):
         total = coupling[0, m] * forcing[0, rows]
         for q in range(1, Q):
@@ -323,13 +355,15 @@
     pack(pushes, pedge_e, pedge_w, 0)
     send_halo(push_halo)
 
+    for i in (0, 6):
+        load(i).wait()
     for m in range(L):
         new_column[m] = column[m] + driven(m, everywhere)
     for q in range(Q):
         total = emission[q, 0] * new_column[0]
         for m in range(1, L):
             total = total + emission[q, m] * new_column[m]
-        next_surface[q] = total
+        partial[q] = total
     await_halo(field_halo)
 
     lane_r = lax.broadcasted_iota(jnp.int32, (ROWS, W), 1)
@@ -349,13 +383,44 @@
         ref = wave.at[i] if i < FAST else fixed.at[i - FAST]
         ref[0] = field_a[i] * scale[i]
         ref[1] = beside(field_e, field_w, i) * scale[i]
-    totals[...] = jnp.zeros_like(totals)
     await_halo(push_halo)
     pscale = [STEP_SIZE, 1.0, 1.0]
     for i in range(FAST):
         fixed[2 + i, 0] = push_a[i] * pscale[i]
         fixed[2 + i, 1] = beside(push_e, push_w, i) * pscale[i]
 
+    for chunk in range(CHUNKS):
+        for mask in range(peers):
+            arrival(mask, chunk).wait_send()
+    drain_halo(field_halo)
+    drain_halo(push_halo)
+
+
+def wave_kernel(
+    bands,
+    new_column,
+    partial,
+    start,
+    fixed,
+    emission_source,
+    column_out,
+    final_out,
+    surface_out,
+    wave,
+    totals,
+    fast_final,
+    next_surface,
+    emission,
+    sems,
+):
+    own = slice(H, 2 * H)
+    up_ok = lax.axis_index("row") < bands - 1
+    load = pltpu.make_async_copy(emission_source, emission, sems.at[0])
+    load.start()
+    column_copy = pltpu.make_async_copy(new_column, column_out, sems.at[1])
+    column_copy.start()
+    wave[...] = start[...]
+    totals[...] = jnp.zeros_like(totals)
     lane8 = lax.broadcasted_iota(jnp.int32, (8, W), 1)
     sub8 = lax.broadcasted_iota(jnp.int32, (8, W), 0)
     west_rim = lane8 == 0
@@ -432,18 +497,20 @@
     back = [1.0 / STEP_SIZE, 1.0, 1.0]
     for i in range(FAST):
         fast_final[i] = wave[i, 0, own] * back[i]
+    final_copy = pltpu.make_async_copy(fast_final, final_out, sems.at[2])
+    final_copy.start()
+    load.wait()
     mean = [totals[i] * (back[i] / SUBSTEPS) for i in range(FAST)]
     for q in range(Q):
-        total = next_surface[q]
+        total = partial[q]
         for i in range(FAST):
             total = total + emission[q, L + i] * mean[i]
         next_surface[q] = jnp.tanh(total)
-
-    for chunk in range(CHUNKS):
-        for mask in range(peers):
-            arrival(mask, chunk).wait_send()
-    drain_halo(field_halo)
-    drain_halo(push_halo)
+    surface_copy = pltpu.make_async_copy(next_surface, surface_out, sems.at[3])
+    surface_copy.start()
+    surface_copy.wait()
+    final_copy.wait()
+    column_copy.wait()
 
 
 def solution(mesh):
@@ -465,18 +532,30 @@
     ):
         f32 = jnp.float32
         vmem = pl.BlockSpec(memory_space=pltpu.VMEM)
-        smem = pl.BlockSpec(memory_space=pltpu.SMEM)
+        hbm = pl.BlockSpec(memory_space=pltpu.HBM)
         dma = pltpu.SemaphoreType.DMA
-        outs = pl.pallas_call(
+        small_emission = emission[0]
+        mid = pl.pallas_call(
             functools.partial(kernel, peers, bands),
             out_shape=(
-                jax.ShapeDtypeStruct((L, H, W), f32),
-                jax.ShapeDtypeStruct((FAST, H, W), f32),
-                jax.ShapeDtypeStruct((Q, H, W), f32),
+                pltpu.VMEM((L, H, W), f32),
+                pltpu.VMEM((Q, H, W), f32),
+                pltpu.VMEM((FAST, 2, ROWS, W), f32),
+                pltpu.VMEM((5, 2, ROWS, W), f32),
             ),
-            in_specs=[vmem] * 5 + [smem] * 2 + [vmem] * 3,
-            out_specs=(vmem, vmem, vmem),
+            in_specs=[hbm] * 10,
+            out_specs=(vmem,) * 4,
             scratch_shapes=[
+                pltpu.VMEM((L, H, W), f32),
+                pltpu.VMEM((FAST, H, W), f32),
+                pltpu.VMEM((H, W), f32),
+                pltpu.VMEM((H, W), jnp.int32),
+                pltpu.VMEM((Q, H, W), f32),
+                pltpu.SMEM(coupling.shape[:0:-1], f32),
+                pltpu.SMEM(emission.shape[1:], f32),
+                pltpu.VMEM((H * K * SPAN, W), jnp.bfloat16),
+                pltpu.VMEM(send_block.shape[2:], jnp.int32),
+                pltpu.VMEM(link_slot.shape[1:], jnp.int32),
                 pltpu.VMEM((head + Q * H, W), jnp.bfloat16),
                 pltpu.VMEM((peers, head + Q * H, W), jnp.bfloat16),
                 pltpu.VMEM((head, W), f32),
@@ -494,9 +573,7 @@
                 pltpu.VMEM((1, ROWS, W), f32),
                 pltpu.VMEM((1, H, W), f32),
                 pltpu.VMEM((1, H, W), f32),
-                pltpu.VMEM((FAST, 2, ROWS, W), f32),
-                pltpu.VMEM((5, 2, ROWS, W), f32),
-                pltpu.VMEM((FAST, H, W), f32),
+                dma((10,)),
                 dma((peers * CHUNKS,)),
                 dma((peers * CHUNKS,)),
                 dma((8,)),
@@ -508,17 +585,36 @@
                 collective_id=0, has_side_effects=True, vmem_limit_bytes=40 << 20
             ),
         )(
-            column[0],
+*[pltpu.with_memory_space_constraint(x, pltpu.HBM) for x in (column[0],
             fast_state[0],
             wave_depth[0],
             wet_mask[0],
             surface[0],
             coupling[0].T,
-            emission[0],
+            small_emission,
             remap_weight.reshape(H * K * SPAN, W),
             send_block[0, 0],
-            link_slot[0],
+            link_slot[0],)]
         )
+        outs = pl.pallas_call(
+            functools.partial(wave_kernel, bands),
+            out_shape=(
+                jax.ShapeDtypeStruct((L, H, W), f32),
+                jax.ShapeDtypeStruct((FAST, H, W), f32),
+                jax.ShapeDtypeStruct((Q, H, W), f32),
+            ),
+            in_specs=[vmem] * 4 + [hbm],
+            out_specs=(hbm,) * 3,
+            scratch_shapes=[
+                pltpu.VMEM((FAST, 2, ROWS, W), f32),
+                pltpu.VMEM((FAST, H, W), f32),
+                pltpu.VMEM((FAST, H, W), f32),
+                pltpu.VMEM((Q, H, W), f32),
+                pltpu.SMEM(emission.shape[1:], f32),
+                dma((4,)),
+            ],
+            compiler_params=pltpu.CompilerParams(vmem_limit_bytes=16 << 20),
+        )(*mid, small_emission)
         return tuple(out[None] for out in outs)
 
     placed = (

time: 33.4 us -> 25.8 us (0.77)
  local copies, waits for them, and re-layouts: 8.23 us -> 0.68 us
    unnamed x23 -> x2, local copies, waits for them, and re-layouts: 8.23 us -> 0.68 us
    pallas_call x1 -> x2, Pallas kernels: 24.1 us -> 24.3 us  [the longest x1 18.1 us: body(): pl.pallas_call(functools.partial(kernel, peers, bands), out_shape=(pltpu....]
where the time goes in v2:
time: 25.8 us; the launch traced here: 25.7 us
  Pallas kernels  24.3 us (94%)
  local copies, waits for them, and re-layouts  0.68 us (3%)
  between operations  0.65 us (3%)
    pallas_call x1, Pallas kernels, body(): pl.pallas_call(functools.partial(kernel, peers, bands), out_shape=(pltpu....  18.1 us
    pallas_call x1, Pallas kernels, body(): pl.pallas_call(functools.partial(wave_kernel, bands), out_shape=(jax.Shap...  6.22 us
    unnamed x2, local copies, waits for them, and re-layouts  0.68 us

profile of v2, /device:TPU:0, one launch (start us, length us, event | category | flops | bytes accessed | tf_op | source)
XLA Modules:
  0.0 25.7 jit_solution(17236163725290780363)
XLA Ops:
  0.6 18.1 %shard_map.121 = (f32[8,32,128]{2,1,0:T(8,128)S(1)}, f32[8,32,128]{2,1,0:T(8,128)S(1)}, f32[3,2,96,128]{3,2,1,0:T(8,128)S(1)}, f32[5,2,96,128]{3,2,1,0:T(8,128)S(1)}) custom-call(f32[8,32,128]{2,1,0:T(8,128)} %bitcast.17, f32[3,32,128]{2,1,0:T(8,128)} %bitcast.20, f32[32,128]{1,0:T(8,128)} %bitcast.21, s32[32,128]{1,0:T(8,128)} %bitcast.22, ...), custom_call_target="tpu_custom_call" | custom-call | tf_op jit(solution)/shard_map/pallas_call | solution.py:538
  18.7 0.0 copy-start
  18.8 0.7 %copy-done = f32[1,8,11]{2,1,0:T(8,128)S(1)} copy-done((f32[1,8,11]{2,1,0:T(8,128)S(1)}, f32[1,8,11]{2,1,0:T(8,128)}, u32[]{:S(2)}) %copy-start) | copy-done | bytes 376
  19.4 6.2 %shard_map.122 = (f32[8,32,128]{2,1,0:T(8,128)}, f32[3,32,128]{2,1,0:T(8,128)}, f32[8,32,128]{2,1,0:T(8,128)}) custom-call(f32[8,32,128]{2,1,0:T(8,128)S(1)} %get-tuple-element.10.new_column, f32[8,32,128]{2,1,0:T(8,128)S(1)} %get-tuple-element.11.partial, f32[3,2,96,128]{3,2,1,0:T(8,128)S(1)} %get-tuple-element.12.start, ...), custom_call_target="tpu_custom_call" | custom-call | tf_op jit(solution)/shard_map/pallas_call | solution.py:599
Async XLA Ops:
  18.7 0.7 %copy-start = (f32[1,8,11]{2,1,0:T(8,128)S(1)}, f32[1,8,11]{2,1,0:T(8,128)}, u32[]{:S(2)}) copy-start(f32[1,8,11]{2,1,0:T(8,128)} %param.16) | copy-start | bytes 1060

commit v3 on v2

--- a/solution.py
+++ b/solution.py
@@ -237,15 +237,15 @@
             last = cells if turn == 0 else pltpu.roll(cells, turn, 1)
             low = jnp.where(here, first, low)
             high = jnp.where(here, last, high)
-        west[tile] = low
-        east[tile] = high
+        west[tile] = low.astype(jnp.bfloat16)
+        east[tile] = high.astype(jnp.bfloat16)
 
     own = slice(H, 2 * H)
     for i in (1, 2):
         load(i).wait()
     statics = [fast_state[i] for i in range(FAST)] + [depth[...], wet]
     for i, cells in enumerate(statics):
-        field_a[i, own] = cells
+        field_a[i, own] = cells.astype(jnp.bfloat16)
     pack(statics[:4], edge_e, edge_w, 0)
     pack(statics[4:], edge_e, edge_w, 1)
 
@@ -351,7 +351,7 @@
     everywhere = slice(0, H)
     pushes = [driven(L + i, everywhere) * (1.0 / SUBSTEPS) for i in range(FAST)]
     for i in range(FAST):
-        push_a[i, own] = pushes[i]
+        push_a[i, own] = pushes[i].astype(jnp.bfloat16)
     pack(pushes, pedge_e, pedge_w, 0)
     send_halo(push_halo)
 
@@ -370,10 +370,10 @@
 
     def beside(east, west, i):
         tile, place = divmod(i, W // PART)
-        near = east[tile]
+        near = east[tile].astype(jnp.float32)
         near = near if place == 0 else pltpu.roll(near, (W - place * PART) % W, 1)
         turn = (W - PART - place * PART) % W
-        far = west[tile]
+        far = west[tile].astype(jnp.float32)
         far = far if turn == 0 else pltpu.roll(far, turn, 1)
         cells = jnp.where(lane_r < PART, near, 0.0)
         return jnp.where(lane_r >= W - PART, far, cells)
@@ -381,12 +381,16 @@
     scale = [STEP_SIZE, 1.0, 1.0, STEP_SIZE * STEP_SIZE, 1.0]
     for i in range(5):
         ref = wave.at[i] if i < FAST else fixed.at[i - FAST]
-        ref[0] = field_a[i] * scale[i]
+        for rows in (slice(0, H), slice(2 * H, ROWS)):
+            ref[0, rows] = field_a[i, rows].astype(jnp.float32) * scale[i]
+        ref[0, own] = statics[i] * scale[i]
         ref[1] = beside(field_e, field_w, i) * scale[i]
     await_halo(push_halo)
     pscale = [STEP_SIZE, 1.0, 1.0]
     for i in range(FAST):
-        fixed[2 + i, 0] = push_a[i] * pscale[i]
+        for rows in (slice(0, H), slice(2 * H, ROWS)):
+            fixed[2 + i, 0, rows] = push_a[i, rows].astype(jnp.float32) * pscale[i]
+        fixed[2 + i, 0, own] = pushes[i] * pscale[i]
         fixed[2 + i, 1] = beside(push_e, push_w, i) * pscale[i]
 
     for chunk in range(CHUNKS):
@@ -406,8 +410,8 @@
     column_out,
     final_out,
     surface_out,
-    wave,
-    totals,
+    even,
+    odd,
     fast_final,
     next_surface,
     emission,
@@ -419,8 +423,7 @@
     load.start()
     column_copy = pltpu.make_async_copy(new_column, column_out, sems.at[1])
     column_copy.start()
-    wave[...] = start[...]
-    totals[...] = jnp.zeros_like(totals)
+    even[...] = start[...]
     lane8 = lax.broadcasted_iota(jnp.int32, (8, W), 1)
     sub8 = lax.broadcasted_iota(jnp.int32, (8, W), 0)
     west_rim = lane8 == 0
@@ -429,7 +432,8 @@
     north_rim = sub8 == 7
     top = jnp.where(up_ok, 1.0, 0.0).astype(jnp.float32)
 
-    def sweep(low, high):
+    def sweep(wave, after, totals, low, high):
+        totals = list(totals)
         south_prev = [jnp.zeros((8, W), jnp.float32)] * 2
         held = None
         for block in range(low, high + 2):
@@ -454,11 +458,10 @@
                     )
                     if block == 2 * H // 8:
                         level = level * top
-                    wave[0, t, rows] = level
+                    after[0, t, rows] = level
                     high_new.append(level)
                 if 4 <= block < 8:
-                    orows = slice(8 * block - H, 8 * block - H + 8)
-                    totals[0, orows] += high_new[0]
+                    totals[block - 4] = totals[block - 4] + high_new[0]
                 south_prev = lifted
                 down = [pltpu.roll(high_new[t], 7, 0) for t in range(2)]
                 now = (rows, block, high_new, flow_e, flow_n, down)
@@ -478,25 +481,28 @@
                     north = open_cells * (
                         DAMPING * flow_n[t] - (to_north - level[t]) + fixed[4, t, rows]
                     )
-                    wave[1, t, rows] = east
-                    wave[2, t, rows] = north
+                    after[1, t, rows] = east
+                    after[2, t, rows] = north
                     if t == 0 and 4 <= block_h < 8:
-                        orows = slice(8 * block_h - H, 8 * block_h - H + 8)
-                        totals[1, orows] += east
-                        totals[2, orows] += north
+                        totals[block_h] = totals[block_h] + east
+                        totals[block_h + 4] = totals[block_h + 4] + north
             held = now
-
+        return tuple(totals)
+
+    sums = (jnp.zeros((8, W), jnp.float32),) * (FAST * H // 8)
     for group in range(SUBSTEPS // 8):
 
-        def step(_, carry, group=group):
-            sweep(group, ROWS // 8 - 1 - group)
-            return carry
-
-        lax.fori_loop(0, 8, step, 0)
+        def steps(_, sums, group=group):
+            low, high = group, ROWS // 8 - 1 - group
+            sums = sweep(even, odd, sums, low, high)
+            return sweep(odd, even, sums, low, high)
+
+        sums = lax.fori_loop(0, 4, steps, sums)
+    totals = [jnp.concatenate(sums[4 * i : 4 * i + 4], axis=0) for i in range(FAST)]
 
     back = [1.0 / STEP_SIZE, 1.0, 1.0]
     for i in range(FAST):
-        fast_final[i] = wave[i, 0, own] * back[i]
+        fast_final[i] = even[i, 0, own] * back[i]
     final_copy = pltpu.make_async_copy(fast_final, final_out, sems.at[2])
     final_copy.start()
     load.wait()
@@ -534,7 +540,7 @@
         vmem = pl.BlockSpec(memory_space=pltpu.VMEM)
         hbm = pl.BlockSpec(memory_space=pltpu.HBM)
         dma = pltpu.SemaphoreType.DMA
-        small_emission = emission[0]
+        small_emission = pltpu.with_memory_space_constraint(emission[0], pltpu.HBM)
         mid = pl.pallas_call(
             functools.partial(kernel, peers, bands),
             out_shape=(
@@ -563,16 +569,16 @@
                 pltpu.VMEM((K * SPAN, H, W), f32),
                 pltpu.VMEM((H * K, 2 * W), f32),
                 pltpu.VMEM((Q, H, W), f32),
-                pltpu.VMEM((5, ROWS, W), f32),
-                pltpu.VMEM((2, ROWS, W), f32),
-                pltpu.VMEM((2, ROWS, W), f32),
-                pltpu.VMEM((2, H, W), f32),
-                pltpu.VMEM((2, H, W), f32),
-                pltpu.VMEM((FAST, ROWS, W), f32),
-                pltpu.VMEM((1, ROWS, W), f32),
-                pltpu.VMEM((1, ROWS, W), f32),
-                pltpu.VMEM((1, H, W), f32),
-                pltpu.VMEM((1, H, W), f32),
+                pltpu.VMEM((5, ROWS, W), jnp.bfloat16),
+                pltpu.VMEM((2, ROWS, W), jnp.bfloat16),
+                pltpu.VMEM((2, ROWS, W), jnp.bfloat16),
+                pltpu.VMEM((2, H, W), jnp.bfloat16),
+                pltpu.VMEM((2, H, W), jnp.bfloat16),
+                pltpu.VMEM((FAST, ROWS, W), jnp.bfloat16),
+                pltpu.VMEM((1, ROWS, W), jnp.bfloat16),
+                pltpu.VMEM((1, ROWS, W), jnp.bfloat16),
+                pltpu.VMEM((1, H, W), jnp.bfloat16),
+                pltpu.VMEM((1, H, W), jnp.bfloat16),
                 dma((10,)),
                 dma((peers * CHUNKS,)),
                 dma((peers * CHUNKS,)),
@@ -607,7 +613,7 @@
             out_specs=(hbm,) * 3,
             scratch_shapes=[
                 pltpu.VMEM((FAST, 2, ROWS, W), f32),
-                pltpu.VMEM((FAST, H, W), f32),
+                pltpu.VMEM((FAST, 2, ROWS, W), f32),
                 pltpu.VMEM((FAST, H, W), f32),
                 pltpu.VMEM((Q, H, W), f32),
                 pltpu.SMEM(emission.shape[1:], f32),

time: 25.8 us -> 23.7 us (0.919)
  Pallas kernels: 24.3 us -> 22.9 us
  local copies, waits for them, and re-layouts: 0.68 us -> 0 us
    pallas_call x1, Pallas kernels: 18.1 us -> 17 us  [body(): pl.pallas_call(functools.partial(kernel, peers, bands), out_shape=(pltpu....]
    unnamed x2 -> x0, local copies, waits for them, and re-layouts: 0.68 us -> none
    pallas_call x1, Pallas kernels: 6.22 us -> 5.92 us  [body(): pl.pallas_call(functools.partial(wave_kernel, bands), out_shape=(jax.Shap...]
where the time goes in v3:
time: 23.7 us; the launch traced here: 23.6 us
  Pallas kernels  22.9 us (97%)
  between operations  0.64 us (3%)
    pallas_call x1, Pallas kernels, body(): pl.pallas_call(functools.partial(kernel, peers, bands), out_shape=(pltpu....  17 us
    pallas_call x1, Pallas kernels, body(): pl.pallas_call(functools.partial(wave_kernel, bands), out_shape=(jax.Shap...  5.92 us

profile of v3, /device:TPU:0, one launch (start us, length us, event | category | flops | bytes accessed | tf_op | source)
XLA Modules:
  0.0 23.6 jit_solution(17649697073564793991)
XLA Ops:
  0.6 17.0 %shard_map.121 = (f32[8,32,128]{2,1,0:T(8,128)S(1)}, f32[8,32,128]{2,1,0:T(8,128)S(1)}, f32[3,2,96,128]{3,2,1,0:T(8,128)S(1)}, f32[5,2,96,128]{3,2,1,0:T(8,128)S(1)}) custom-call(f32[8,32,128]{2,1,0:T(8,128)} %bitcast.15, f32[3,32,128]{2,1,0:T(8,128)} %bitcast.18, f32[32,128]{1,0:T(8,128)} %bitcast.21, s32[32,128]{1,0:T(8,128)} %bitcast.22, ...), custom_call_target="tpu_custom_call" | custom-call | tf_op jit(solution)/shard_map/pallas_call | solution.py:544
  17.6 5.9 %shard_map.122 = (f32[8,32,128]{2,1,0:T(8,128)}, f32[3,32,128]{2,1,0:T(8,128)}, f32[8,32,128]{2,1,0:T(8,128)}) custom-call(f32[8,32,128]{2,1,0:T(8,128)S(1)} %get-tuple-element.10.new_column, f32[8,32,128]{2,1,0:T(8,128)S(1)} %get-tuple-element.11.partial, f32[3,2,96,128]{3,2,1,0:T(8,128)S(1)} %get-tuple-element.12.start, ...), custom_call_target="tpu_custom_call" | custom-call | tf_op jit(solution)/shard_map/pallas_call | solution.py:605

commit v4 on v3

--- a/solution.py
+++ b/solution.py
@@ -210,8 +210,8 @@
     field_halo = (field_a, edge_e, edge_w, field_e, field_w, field_send, field_recv)
     push_halo = (push_a, pedge_e, pedge_w, push_e, push_w, push_send, push_recv)
 
-    def send_halo(halo):
-        for dr, dc in TURNS:
+    def send_halo(halo, turns):
+        for dr, dc in turns:
             guarded(dr, lambda dr=dr, dc=dc: halo_copy(dr, dc, *halo).start())
 
     def await_halo(halo):
@@ -237,15 +237,15 @@
             last = cells if turn == 0 else pltpu.roll(cells, turn, 1)
             low = jnp.where(here, first, low)
             high = jnp.where(here, last, high)
-        west[tile] = low.astype(jnp.bfloat16)
-        east[tile] = high.astype(jnp.bfloat16)
+        west[tile] = low.astype(west.dtype)
+        east[tile] = high.astype(east.dtype)
 
     own = slice(H, 2 * H)
     for i in (1, 2):
         load(i).wait()
     statics = [fast_state[i] for i in range(FAST)] + [depth[...], wet]
     for i, cells in enumerate(statics):
-        field_a[i, own] = cells.astype(jnp.bfloat16)
+        field_a[i, own] = cells
     pack(statics[:4], edge_e, edge_w, 0)
     pack(statics[4:], edge_e, edge_w, 1)
 
@@ -259,7 +259,7 @@
         for ref in (field_a, field_e, field_w, push_a, push_e, push_w):
             ref[:, 2 * H : 3 * H] = jnp.zeros_like(ref[:, 2 * H : 3 * H])
 
-    send_halo(field_halo)
+    send_halo(field_halo, TURNS)
 
     load(7).wait()
     wide[...] = weights[...].astype(jnp.float32)
@@ -352,8 +352,9 @@
     pushes = [driven(L + i, everywhere) * (1.0 / SUBSTEPS) for i in range(FAST)]
     for i in range(FAST):
         push_a[i, own] = pushes[i].astype(jnp.bfloat16)
+    send_halo(push_halo, [turn for turn in TURNS if turn[1] == 0])
     pack(pushes, pedge_e, pedge_w, 0)
-    send_halo(push_halo)
+    send_halo(push_halo, [turn for turn in TURNS if turn[1] != 0])
 
     for i in (0, 6):
         load(i).wait()
@@ -497,7 +498,7 @@
             sums = sweep(even, odd, sums, low, high)
             return sweep(odd, even, sums, low, high)
 
-        sums = lax.fori_loop(0, 4, steps, sums)
+        sums = lax.fori_loop(0, 4, steps, sums, unroll=2)
     totals = [jnp.concatenate(sums[4 * i : 4 * i + 4], axis=0) for i in range(FAST)]
 
     back = [1.0 / STEP_SIZE, 1.0, 1.0]
@@ -569,11 +570,11 @@
                 pltpu.VMEM((K * SPAN, H, W), f32),
                 pltpu.VMEM((H * K, 2 * W), f32),
                 pltpu.VMEM((Q, H, W), f32),
-                pltpu.VMEM((5, ROWS, W), jnp.bfloat16),
-                pltpu.VMEM((2, ROWS, W), jnp.bfloat16),
-                pltpu.VMEM((2, ROWS, W), jnp.bfloat16),
-                pltpu.VMEM((2, H, W), jnp.bfloat16),
-                pltpu.VMEM((2, H, W), jnp.bfloat16),
+                pltpu.VMEM((5, ROWS, W), f32),
+                pltpu.VMEM((2, ROWS, W), f32),
+                pltpu.VMEM((2, ROWS, W), f32),
+                pltpu.VMEM((2, H, W), f32),
+                pltpu.VMEM((2, H, W), f32),
                 pltpu.VMEM((FAST, ROWS, W), jnp.bfloat16),
                 pltpu.VMEM((1, ROWS, W), jnp.bfloat16),
                 pltpu.VMEM((1, ROWS, W), jnp.bfloat16),

time: 23.7 us -> 23.6 us (level)
  no operation moved by 1% of the time
where the time goes in v4:
time: 23.6 us; the launch traced here: 23.5 us
  Pallas kernels  22.9 us (97%)
  between operations  0.64 us (3%)
    pallas_call x1, Pallas kernels, body(): pl.pallas_call(functools.partial(kernel, peers, bands), out_shape=(pltpu....  17.1 us
    pallas_call x1, Pallas kernels, body(): pl.pallas_call(functools.partial(wave_kernel, bands), out_shape=(jax.Shap...  5.72 us

profile of v4, /device:TPU:0, one launch (start us, length us, event | category | flops | bytes accessed | tf_op | source)
XLA Modules:
  0.0 23.5 jit_solution(2360451817118852096)
XLA Ops:
  0.6 17.1 %shard_map.121 = (f32[8,32,128]{2,1,0:T(8,128)S(1)}, f32[8,32,128]{2,1,0:T(8,128)S(1)}, f32[3,2,96,128]{3,2,1,0:T(8,128)S(1)}, f32[5,2,96,128]{3,2,1,0:T(8,128)S(1)}) custom-call(f32[8,32,128]{2,1,0:T(8,128)} %bitcast.15, f32[3,32,128]{2,1,0:T(8,128)} %bitcast.18, f32[32,128]{1,0:T(8,128)} %bitcast.21, s32[32,128]{1,0:T(8,128)} %bitcast.22, ...), custom_call_target="tpu_custom_call" | custom-call | tf_op jit(solution)/shard_map/pallas_call | solution.py:545
  17.8 5.7 %shard_map.122 = (f32[8,32,128]{2,1,0:T(8,128)}, f32[3,32,128]{2,1,0:T(8,128)}, f32[8,32,128]{2,1,0:T(8,128)}) custom-call(f32[8,32,128]{2,1,0:T(8,128)S(1)} %get-tuple-element.10.new_column, f32[8,32,128]{2,1,0:T(8,128)S(1)} %get-tuple-element.11.partial, f32[3,2,96,128]{3,2,1,0:T(8,128)S(1)} %get-tuple-element.12.start, ...), custom_call_target="tpu_custom_call" | custom-call | tf_op jit(solution)/shard_map/pallas_call | solution.py:606
